TPU v7x, 32 devices: a whole 2x2x4 slice. The times are simulated.
32 devices in a mesh: groups: 2 (over x), blk: 16 (over z, y, core).
Axes of the slice: x: 2, y: 2, z: 4, core: 2. Of those that a mesh axis runs over, the one named last changes fastest.
Arguments:
- image_feats: bfloat16 [4096, 768], P(('groups', 'blk')), parts along dimension 0, may hold values from -32 to 32
- text_feats: bfloat16 [4096, 512], P(('groups', 'blk')), parts along dimension 0, may hold values from -32 to 32
- class_ids: int32 [4096], P(('groups', 'blk')), parts along dimension 0, may hold values from 0 to 2047
- w_img: bfloat16 [768, 512], replicated, may hold values from -1 to 1
- w_txt: bfloat16 [512, 512], replicated, may hold values from -1 to 1
Outputs:
- loss: float32 [2], P('groups'), parts along dimension 0
- grad_w_img: float32 [1536, 512], P('groups'), parts along dimension 0
- grad_w_txt: float32 [1024, 512], P('groups'), parts along dimension 0
There are 2 independent parts, one for each index of `groups`. A program takes and returns all parts, laid end to end along the dimension named above; an argument that names none is the same for every part. Nothing has to cross between parts.
All inputs are finite; a program needn't handle non-finite values.
Results may differ from a plain program's by a relative error of at most 0.0021.
Values may be sent and summed in bfloat16 or wider, within the bound.
A program may use at most 64 MiB of HBM per device.

v0:
```python
import jax
import jax.numpy as jnp
from jax import lax
from jax.sharding import PartitionSpec as P

LOGIT_SCALE = 10.0
LOGIT_BIAS = -10.0
NORM_EPS = 1e-06


def second_term(dot_buffer, scaled_txt, unit_txt):
    exact = lax.Precision.HIGHEST
    row_dot = lax.psum_scatter(dot_buffer, "blk", scatter_dimension=0, tiled=True)
    return jnp.dot(scaled_txt.astype(jnp.float32).T, unit_txt * row_dot[:, None], precision=exact)


def body(image_feats, text_feats, class_ids, w_img, w_txt):
    exact = lax.Precision.HIGHEST
    own_rows = image_feats.shape[0]
    all_rows = own_rows * lax.axis_size("blk")
    proj_img = jnp.dot(image_feats, w_img, preferred_element_type=jnp.float32)
    inv_img = lax.rsqrt(jnp.sum(proj_img * proj_img, axis=1, keepdims=True) + NORM_EPS)
    unit_img = proj_img * inv_img
    proj_txt = jnp.dot(text_feats, w_txt, preferred_element_type=jnp.float32)
    inv_txt = lax.rsqrt(jnp.sum(proj_txt * proj_txt, axis=1, keepdims=True) + NORM_EPS)
    scaled_txt = (text_feats.astype(jnp.float32) * inv_txt).astype(jnp.bfloat16)
    txt_weight = w_txt.astype(jnp.float32)
    query_rows = jnp.dot(unit_img, txt_weight.T, precision=exact).astype(jnp.bfloat16)

    def visit(state_now, shard_rows, shard_ids, offset):
        loss_sum, across_sum, back_sum, dot_buffer = state_now
        cosine = jnp.dot(query_rows, shard_rows.T, preferred_element_type=jnp.float32)
        logits = LOGIT_SCALE * cosine + LOGIT_BIAS
        labels = jnp.where(class_ids[:, None] == shard_ids[None, :], 1.0, -1.0).astype(jnp.float32)
        loss_sum = loss_sum + jnp.sum(jax.nn.softplus(-labels * logits))
        slope = -LOGIT_SCALE * labels * jax.nn.sigmoid(-labels * logits) / all_rows
        slope_b = slope.astype(jnp.bfloat16)
        across_sum = across_sum + jnp.dot(slope_b, shard_rows, preferred_element_type=jnp.float32)
        back_sum = back_sum + lax.dot_general(
            shard_rows, slope_b, (((0,), (1,)), ((), ())), preferred_element_type=jnp.float32
        )
        column_dots = jnp.sum(slope * cosine, axis=0)
        dot_buffer = lax.dynamic_update_slice_in_dim(dot_buffer, column_dots, offset, 0)
        return (loss_sum, across_sum, back_sum, dot_buffer)

    start_carry = (
        jnp.zeros((), jnp.float32),
        jnp.zeros((own_rows, scaled_txt.shape[1]), jnp.float32),
        jnp.zeros((scaled_txt.shape[1], own_rows), jnp.float32),
        jnp.zeros((all_rows,), jnp.float32),
    )
    gathered_rows, gathered_ids = (
        lax.all_gather(scaled_txt, "blk", axis=0, tiled=True),
        lax.all_gather(class_ids, "blk", axis=0, tiled=True),
    )
    span_rows = 4 * own_rows
    span_count = all_rows // span_rows

    def loop_step(span_index, state_now):
        offset = span_index * span_rows
        shard_rows = lax.dynamic_slice_in_dim(gathered_rows, offset, span_rows, 0)
        shard_ids = lax.dynamic_slice_in_dim(gathered_ids, offset, span_rows, 0)
        return visit(state_now, shard_rows, shard_ids, offset)

    final_state = lax.fori_loop(0, span_count, loop_step, start_carry)
    loss_sum, across_sum, back_sum, dot_buffer = final_state
    d_unit_img = jnp.dot(across_sum, txt_weight, precision=exact)
    d_proj_img = inv_img * (
        d_unit_img - unit_img * jnp.sum(unit_img * d_unit_img, axis=1, keepdims=True)
    )
    image_grad = jnp.dot(image_feats.astype(jnp.float32).T, d_proj_img, precision=exact)
    text_first = jnp.dot(back_sum, unit_img, precision=exact)
    unit_txt = jnp.dot(scaled_txt, w_txt, preferred_element_type=jnp.float32)
    text_second = second_term(dot_buffer, scaled_txt, unit_txt)
    total_loss, grad_w_img, grad_w_txt = lax.psum(
        (loss_sum, image_grad, text_first - text_second), "blk"
    )
    loss = (total_loss / all_rows).reshape(1)
    return (loss, grad_w_img, grad_w_txt)


def solution(mesh):
    return jax.shard_map(
        body,
        mesh=mesh,
        in_specs=(
            P(("groups", "blk"), None),
            P(("groups", "blk"), None),
            P(("groups", "blk")),
            P(),
            P(),
        ),
        out_specs=(P("groups"), P("groups", None), P("groups", None)),
        check_vma=False,
    )
```

profile of v0, /device:TPU:0, one launch (start us, length us, event | category | flops | bytes accessed | tf_op | source)
XLA Modules:
  0.0 228.5 jit_solution(11415784477957599064)
XLA Ops:
  7.2 1.5 fusion.14
  8.8 1.7 multiply_convert_fusion
  10.5 1.3 dynamic-slice
  12.4 23.2 %all-gather = s32[16,1,128]{2,1,0:T(1,128)S(1)} all-gather(s32[1,1,128]{2,1,0:T(1,128)} %bitcast.25), channel_id=1, replica_groups=mesh['groups'=2,'blk'=16] {'blk'}, dimensions={0}, use_global_device_ids=true | all-gather | bytes 8704 | tf_op jit(solution)/shard_map/all_gather | solution.py:54
  35.6 1.3 multiply_reduce_fusion.2
  37.5 17.4 %all-gather.3.cloned.1.call-done = bf16[2048,512]{1,0:T(8,128)(2,1)} async-done(((bf16[128,512]{1,0:T(8,128)(2,1)}), bf16[2048,512]{1,0:T(8,128)(2,1)}) %all-gather.3.cloned.1.call-update) | async-done | bytes 2097168 | tf_op jit(solution)/shard_map/all_gather | solution.py:53
  54.9 24.5 %while.20 = (s32[]{:T(128)}, f32[]{:T(128)}, f32[128,512]{1,0:T(8,128)S(1)}, f32[512,128]{1,0:T(8,128)S(1)}, f32[2048]{0:T(1024)S(1)}, /*index=5*/s32[128]{0:T(1...) while((s32[]{:T(128)}, f32[]{:T(128)}, ...), condition=%wide.region_5.6_spmd.clone, body=%wide.region_2.5_spmd.clone.sunk | while | flops 204668416 | bytes 3557090 | solution.py:65
  55.0 2.2 multiply_reduce_fusion.4
  58.1 1.5 convolution_add_fusion.5
  59.6 1.4 convolution_add_fusion.4
  61.1 2.2 multiply_reduce_fusion.4
  64.3 1.5 convolution_add_fusion.5
  65.8 1.4 convolution_add_fusion.4
  67.3 2.2 multiply_reduce_fusion.4
  70.4 1.5 convolution_add_fusion.5
  71.9 1.4 convolution_add_fusion.4
  73.4 2.2 multiply_reduce_fusion.4
  76.5 1.5 convolution_add_fusion.5
  78.0 1.4 convolution_add_fusion.4
  79.4 33.4 %all-reduce.1 = (f32[]{:T(128)}, f32[2048]{0:T(1024)S(1)}) all-reduce(f32[]{:T(128)} %get-tuple-element.160, f32[2048]{0:T(1024)S(1)} %get-tuple-element.163), channel_id=1, replica_groups=mesh['groups'=2,'blk'=16] {'blk'}, use_global_device_ids=true, to_apply=%region_6.7 | all-reduce | flops 2049 | bytes 16392 | tf_op jit(solution)/shard_map/psum | solution.py:75
  114.7 1.6 convolution_subtract_fusion
  116.3 2.0 convolution_bitcast_fusion.1
  119.0 97.5 %all-reduce.5.cloned.1.call-done = (f32[768,512]{0,1:T(8,128)}, f32[512,512]{1,0:T(8,128)}) async-done(((f32[768,512]{0,1:T(8,128)}, f32[512,512]{1,0:T(8,128)}), (f32[768,512]{0,1:T(8,128)}, f32[512,512]{1,0:T(8,128)})) %all-reduce.5.cloned.1.call-update) | async-done | bytes 2621456 | tf_op jit(solution)/shard_map/psum | solution.py:75
  216.5 3.1 %copy.9 = f32[768,512]{1,0:T(8,128)} copy(f32[768,512]{0,1:T(8,128)} %get-tuple-element.222) | data formatting | bytes 3145728
  (35 shorter events, 5.0 us)
Async XLA Ops:
  7.2 28.4 %copy-start = (bf16[768,512]{1,0:T(8,128)(2,1)S(1)}, bf16[768,512]{1,0:T(8,128)(2,1)}, u32[]{:S(2)}) copy-start(bf16[768,512]{1,0:T(8,128)(2,1)} %param.10) | copy-start | bytes 2359300
  7.2 29.7 %copy-start.1 = (bf16[512,512]{1,0:T(8,128)(2,1)S(1)}, bf16[512,512]{1,0:T(8,128)(2,1)}, u32[]{:S(2)}) copy-start(bf16[512,512]{1,0:T(8,128)(2,1)} %param.11) | copy-start | bytes 1572868
  7.2 47.7 %copy-start.5 = (s32[128]{0:T(128)S(1)}, s32[128]{0:T(128)}, u32[]{:S(2)}) copy-start(s32[128]{0:T(128)} %param.9) | copy-start | bytes 1540
  7.2 47.7 %all-gather.3.cloned.1.call-start = ((), (), s32[]{:S(2)}) async-start(), calls=%async_computation | async-start | bytes 2228224 | tf_op jit(solution)/shard_map/all_gather | solution.py:53
  10.4 206.0 %all-reduce.5.cloned.1.call-start = ((), (), s32[]{:S(2)}) async-start(), calls=%async_computation.1 | async-start | bytes 5242880 | tf_op jit(solution)/shard_map/psum | solution.py:75
  54.9 58.0 %copy-start.2 = (bf16[128,512]{1,0:T(8,128)(2,1)S(1)}, bf16[128,512]{1,0:T(8,128)(2,1)}, u32[]{:S(2)}) copy-start(bf16[128,512]{1,0:T(8,128)(2,1)} %multiply_convert_fusion) | copy-start | bytes 393220
  113.6 2.7 %copy-start.4 = (bf16[128,768]{1,0:T(8,128)(2,1)S(1)}, bf16[128,768]{1,0:T(8,128)(2,1)}, u32[]{:S(2)}) copy-start(bf16[128,768]{1,0:T(8,128)(2,1)} %param.7) | copy-start | bytes 589828
  216.5 3.1 %copy-start.3 = (f32[512,512]{1,0:T(8,128)S(1)}, f32[512,512]{1,0:T(8,128)}, u32[]{:S(2)}) copy-start(f32[512,512]{1,0:T(8,128)} %get-tuple-element.331) | copy-start | bytes 3145732
Sparse Core Ops, SparseCore 0:
  10.8 44.1 all-gather.2
  118.5 97.9 all-reduce.4
where the time goes:
time: 229 us
  waiting for transfers between devices  115 us (50%)
  blocking collectives  56.6 us (25%)
  matrix products  29.3 us (13%)
  between operations  16.6 us (7%)
  local copies, waits for them, and re-layouts  6.82 us (3%)
  loops' own time  2.63 us (1%)
    psum x1, waiting for transfers between devices, body(): lax.psum((loss_sum, image_grad, text_first - text_second), 'blk')  97.5 us
    psum x1, blocking collectives, body(): lax.psum((loss_sum, image_grad, text_first - text_second), 'blk')  33.4 us
    all_gather x1, blocking collectives, body(): lax.all_gather(class_ids, 'blk', axis=0, tiled=True)  23.2 us
    all_gather x1, waiting for transfers between devices, body(): lax.all_gather(scaled_txt, 'blk', axis=0, tiled=True)  17.4 us
    dot_general x4, matrix products, visit(): jnp.dot(query_rows, shard_rows.T, preferred_element_type=jnp.float32)  8.88 us
    dot_general x4, matrix products, visit(): lax.dot_general(shard_rows, slope_b, (((0,), (1,)), ((), ())), preferred_...  6.01 us
    dot_general x4, matrix products, visit(): jnp.dot(slope_b, shard_rows, preferred_element_type=jnp.float32)  5.57 us
    unnamed x16, local copies, waits for them, and re-layouts  5.44 us
  transfers between devices with their start and end apart: 2, of which 2 were waited for; matrix products, arithmetic and copies ran while one was open for 1% of the time, Pallas kernels for 0%

commit v1 on v0

v1 whole, which is shorter than its diff:
```python
import functools

import jax
import jax.numpy as jnp
from jax import lax
from jax.experimental import pallas as pl
from jax.experimental.pallas import tpu as pltpu
from jax.sharding import PartitionSpec as P

LOGIT_SCALE = 10.0
LOGIT_BIAS = -10.0
NORM_EPS = 1e-06
F32 = jnp.float32
BF16 = jnp.bfloat16
LEVELS = 32767.0


def grid_of(n):
    chips = n // 2
    fast = 1
    while fast * fast * 4 <= chips and chips % (fast * 2) == 0:
        fast *= 2
    return chips // fast, fast


def chunk_rows(rows, n):
    slow, fast = grid_of(n)
    part = rows // (2 * fast)
    return part, -(-part // (slow * 16)) * 16


def split(value):
    high = value.astype(BF16)
    return high, (value - high.astype(F32)).astype(BF16)


def quantize(value):
    peak = jnp.maximum(jnp.max(jnp.abs(value), axis=0, keepdims=True), 1e-30)
    return jnp.round(value * (LEVELS / peak)).astype(jnp.int32).astype(jnp.int16), peak / LEVELS


def dequantize(value, scale):
    return value.astype(jnp.int32).astype(F32) * scale


def dot_nn(a, b):
    return jnp.dot(a, b, preferred_element_type=F32)


def dot_nt(a, b):
    return lax.dot_general(a, b, (((1,), (1,)), ((), ())), preferred_element_type=F32)


def dot_tn(a, b):
    return lax.dot_general(a, b, (((0,), (0,)), ((), ())), preferred_element_type=F32)


def as_column(row):
    length = row.shape[1]
    return jnp.broadcast_to(row, (length, length)).T[:, :1]


def kernel(
    n,
    img_ref, txt_ref, ids_ref, w_img_ref, w_txt_ref,
    loss_ref, full_ref, scale_ref,
    rows_all, ids_all, message, arrived, across_ref, loss_acc, grads,
    out_core, in_core, out_fast, in_fast, own_part, out_slow, in_slow,
    out_core_scale, in_core_scale, out_fast_scale, in_fast_scale, out_slow_scale, in_slow_scale,
    rows_send, rows_recv, ids_sem, msg_sem, core_sem, fast_sem, slow_sem, full_send, full_recv,
    scale_sem,
):
    slow, fast = grid_of(n)
    chunk = full_ref.shape[1]
    part = (img_ref.shape[1] + txt_ref.shape[1]) // (2 * fast)
    own = img_ref.shape[0]
    total_rows = n * own
    me = lax.axis_index("blk")
    mc = lax.rem(me, 2)
    my = lax.rem(me // 2, fast)
    mz = me // (2 * fast)

    def device(z, y, c):
        return (z * fast + y) * 2 + c

    sibling = device(mz, my, 1 - mc)

    barrier = pltpu.get_barrier_semaphore()

    def greet(i, carry):
        pl.semaphore_signal(barrier, inc=1, device_id={"blk": lax.rem(me + i, n)})
        return carry

    lax.fori_loop(1, n, greet, 0)

    proj_txt = dot_nn(txt_ref[...], w_txt_ref[...])
    inv_txt = lax.rsqrt(jnp.sum(proj_txt * proj_txt, axis=1, keepdims=True) + NORM_EPS)
    rows_all[me] = (txt_ref[...].astype(F32) * inv_txt).astype(BF16)
    ids_all[me] = ids_ref[...]

    pl.semaphore_wait(barrier, n - 1)

    def spread(buffer, slot, send_sem, recv_sem, use):
        def copy(z, y, c, dst, k):
            return pltpu.make_async_remote_copy(
                src_ref=buffer.at[slot(z, y, c)],
                dst_ref=buffer.at[slot(z, y, c)],
                send_sem=send_sem.at[k],
                recv_sem=recv_sem.at[device(z, y, c)],
                device_id={"blk": dst},
            )

        base = slow - 1
        last = base + slow * (fast - 1)

        for dy in range(1, fast):
            copy(mz, my, mc, device(mz, lax.rem(my + dy, fast), mc), base + dy - 1).start()
        for dz in range(1, slow):
            copy(mz, my, mc, device(lax.rem(mz + dz, slow), my, mc), dz - 1).start()
        copy(mz, my, mc, sibling, last).start()

        def step(t, carry):
            dz, dy = t // fast, lax.rem(t, fast)
            z, y = lax.rem(mz + dz, slow), lax.rem(my + dy, fast)

            @pl.when(t > 0)
            def _():
                copy(z, y, mc, sibling, last + t).wait_recv()

                @pl.when(dy == 0)
                def _():
                    for other in range(1, fast):
                        k = base + dz * (fast - 1) + other - 1
                        copy(z, y, mc, device(mz, lax.rem(my + other, fast), mc), k).start()

                copy(z, y, mc, sibling, last + t).start()

            copy(z, y, 1 - mc, sibling, 0).wait_recv()
            use(z * fast + y)
            return carry

        lax.fori_loop(0, slow * fast, step, 0)

        def drain(k, carry):
            copy(mz, my, mc, sibling, k).wait_send()
            return carry

        return lambda: lax.fori_loop(0, n - 1, drain, 0)

    def ids_copy(i):
        return pltpu.make_async_remote_copy(
            src_ref=ids_all.at[me],
            dst_ref=ids_all.at[me],
            send_sem=ids_sem.at[0],
            recv_sem=ids_sem.at[1],
            device_id={"blk": lax.rem(me + i, n)},
        )

    def ids_start(i, carry):
        ids_copy(i).start()
        return carry

    lax.fori_loop(1, n, ids_start, 0)
    ids_whole = pltpu.make_async_remote_copy(
        src_ref=ids_all.at[pl.ds(0, n - 1)],
        dst_ref=ids_all.at[pl.ds(0, n - 1)],
        send_sem=ids_sem.at[0],
        recv_sem=ids_sem.at[1],
        device_id={"blk": sibling},
    )

    proj_img = dot_nn(img_ref[...], w_img_ref[...])
    inv_img = lax.rsqrt(jnp.sum(proj_img * proj_img, axis=1, keepdims=True) + NORM_EPS)
    unit_img = proj_img * inv_img
    unit_high, unit_low = split(unit_img)
    query = (dot_nt(unit_high, w_txt_ref[...]) + dot_nt(unit_low, w_txt_ref[...])).astype(BF16)
    unit_txt = dot_nn(rows_all[me], w_txt_ref[...])
    own_ids = as_column(ids_ref[...].astype(F32))

    across_ref[...] = jnp.zeros_like(across_ref)
    loss_acc[...] = jnp.zeros_like(loss_acc)

    def visit(chip):
        @pl.when(chip == me // 2)
        def _():
            ids_whole.wait()

        block = rows_all[pl.ds(2 * chip, 2)].reshape(2 * own, rows_all.shape[2])
        ids = jnp.concatenate([ids_all[2 * chip], ids_all[2 * chip + 1]], axis=1).astype(F32)
        cosine = dot_nt(query, block)
        logits = LOGIT_SCALE * cosine + LOGIT_BIAS
        labels = jnp.where(own_ids == ids, 1.0, -1.0).astype(F32)
        margin = -labels * logits
        decay = jnp.exp(-jnp.abs(margin))
        loss_acc[...] += jnp.sum(jnp.maximum(margin, 0.0) + jnp.log1p(decay), axis=0, keepdims=True)
        gate = jnp.where(margin >= 0.0, 1.0, decay) / (1.0 + decay)
        slope = (-LOGIT_SCALE / total_rows) * labels * gate
        across_ref[...] += dot_nn(slope.astype(BF16), block)
        dots = jnp.sum(slope * cosine, axis=0, keepdims=True)
        message[2 * chip, :, pl.ds(0, own)] = dots[:, :own]
        message[2 * chip + 1, :, pl.ds(0, own)] = dots[:, own:]

    rows_done = spread(rows_all, device, rows_send, rows_recv, visit)

    losses = loss_acc[:, :own] + loss_acc[:, own:]
    message[:, :, pl.ds(own, own)] = jnp.broadcast_to(losses[None], (n, 1, own))
    arrived[me] = message[me]

    def msg_start(i, carry):
        dst = lax.rem(me + i, n)
        pltpu.make_async_remote_copy(
            src_ref=message.at[dst],
            dst_ref=arrived.at[me],
            send_sem=msg_sem.at[0],
            recv_sem=msg_sem.at[1],
            device_id={"blk": dst},
        ).start()
        return carry

    lax.fori_loop(1, n, msg_start, 0)

    def keep(first, value):
        done = 0
        while done < value.shape[0]:
            index, offset = divmod(first + done, part)
            count = min(part - offset, value.shape[0] - done)
            grads[index, pl.ds(offset, count)] = value[done:done + count]
            done += count

    across = across_ref[...]
    across_high, across_low = split(across)
    d_unit_img = dot_nn(across_high, w_txt_ref[...]) + dot_nn(across_low, w_txt_ref[...])
    d_proj_img = inv_img * (
        d_unit_img - unit_img * jnp.sum(unit_img * d_unit_img, axis=1, keepdims=True)
    )
    d_high, d_low = split(d_proj_img)
    img = img_ref[...]
    if slow * chunk > part:
        grads[:, pl.ds(part, slow * chunk - part)] = jnp.zeros(
            (2 * fast, slow * chunk - part, grads.shape[2]), F32
        )
    keep(0, dot_tn(jnp.concatenate([img, img]), jnp.concatenate([d_high, d_low])))

    text_first = dot_tn(
        jnp.concatenate([across_high, across_low, across_high]),
        jnp.concatenate([unit_high, unit_high, unit_low]),
    )
    pltpu.make_async_remote_copy(
        src_ref=message.at[pl.ds(0, n - 1)],
        dst_ref=arrived.at[pl.ds(0, n - 1)],
        send_sem=msg_sem.at[0],
        recv_sem=msg_sem.at[1],
        device_id={"blk": sibling},
    ).wait()
    everything = jnp.sum(arrived[...], axis=0)
    loss_ref[...] = jnp.sum(everything[:, own:], axis=1, keepdims=True) / total_rows
    row_dot = as_column(everything[:, :own])
    text_high, text_low = split(unit_txt * row_dot)
    rows_own = rows_all[me]
    text_second = dot_tn(
        jnp.concatenate([rows_own, rows_own]), jnp.concatenate([text_high, text_low])
    )
    keep(img_ref.shape[1], text_first - text_second)

    class Message:
        def __init__(self, source, target, source_scale, target_scale, sem, index, dst):
            self.source, self.source_scale, self.index = source, source_scale, index
            self.target, self.target_scale = target, target_scale
            self.copies = [
                pltpu.make_async_remote_copy(
                    src_ref=a.at[index],
                    dst_ref=b.at[index],
                    send_sem=sem.at[2 * k, index],
                    recv_sem=sem.at[2 * k + 1, index],
                    device_id={"blk": dst},
                )
                for k, (a, b) in enumerate([(source, target), (source_scale, target_scale)])
            ]

        def send(self, value):
            self.source[self.index], self.source_scale[self.index] = quantize(value)
            for copy in self.copies:
                copy.start()

        def receive(self):
            for copy in self.copies:
                copy.wait_recv()
            return dequantize(self.target[self.index], self.target_scale[self.index])

        def finish(self):
            for copy in self.copies:
                copy.wait_send()

    def core_message(j):
        return Message(out_core, in_core, out_core_scale, in_core_scale, core_sem, j, sibling)

    def fast_message(d):
        dst = device(mz, lax.rem(my + d, fast), mc)
        return Message(out_fast, in_fast, out_fast_scale, in_fast_scale, fast_sem, d - 1, dst)

    def slow_message(d):
        dst = device(lax.rem(mz + d, slow), my, mc)
        return Message(out_slow, in_slow, out_slow_scale, in_slow_scale, slow_sem, d - 1, dst)

    for d in list(range(1, fast)) + [0]:
        j = lax.rem(my + d, fast)
        core_message(j).send(grads[(1 - mc) * fast + j])
    for d in range(1, fast):
        j = lax.rem(my + d, fast)
        fast_message(d).send(grads[mc * fast + j] + core_message(j).receive())
    part_sum = grads[mc * fast + my] + core_message(my).receive()
    for d in range(1, fast):
        part_sum = part_sum + fast_message(d).receive()
    own_part[...] = part_sum.reshape(own_part.shape)
    for d in range(1, slow):
        slow_message(d).send(own_part[lax.rem(mz + d, slow)])
    chunk_sum = own_part[mz]
    for d in range(1, slow):
        chunk_sum = chunk_sum + slow_message(d).receive()

    def place(z, y, c):
        return (c * fast + y) * slow + z

    mine = place(mz, my, mc)
    full_ref[mine], scale_ref[mine] = quantize(chunk_sum)

    def scale_start(i, carry):
        pltpu.make_async_remote_copy(
            src_ref=scale_ref.at[mine],
            dst_ref=scale_ref.at[mine],
            send_sem=scale_sem.at[0],
            recv_sem=scale_sem.at[1],
            device_id={"blk": lax.rem(me + i, n)},
        ).start()
        return carry

    lax.fori_loop(1, n, scale_start, 0)
    full_done = spread(full_ref, place, full_send, full_recv, lambda chip: None)
    pltpu.make_async_remote_copy(
        src_ref=scale_ref.at[pl.ds(0, n - 1)],
        dst_ref=scale_ref.at[pl.ds(0, n - 1)],
        send_sem=scale_sem.at[0],
        recv_sem=scale_sem.at[1],
        device_id={"blk": sibling},
    ).wait()

    rows_done()
    for j in range(fast):
        core_message(j).finish()
    for d in range(1, fast):
        fast_message(d).finish()
    for d in range(1, slow):
        slow_message(d).finish()
    full_done()


def body(n, image_feats, text_feats, class_ids, w_img, w_txt):
    slow, fast = grid_of(n)
    own, wide_img = image_feats.shape
    wide_txt = text_feats.shape[1]
    shared = w_img.shape[1]
    part, chunk = chunk_rows(wide_img + wide_txt, n)
    dma = pltpu.SemaphoreType.DMA
    loss, full, scale = pl.pallas_call(
        functools.partial(kernel, n),
        out_shape=(
            jax.ShapeDtypeStruct((1, 1), F32),
            jax.ShapeDtypeStruct((n, chunk, shared), jnp.int16),
            jax.ShapeDtypeStruct((n, 1, shared), F32),
        ),
        in_specs=[pl.BlockSpec(memory_space=pltpu.VMEM)] * 5,
        out_specs=(pl.BlockSpec(memory_space=pltpu.VMEM),) * 3,
        scratch_shapes=[
            pltpu.VMEM((n, own, wide_txt), BF16),
            pltpu.VMEM((n, 1, own), jnp.int32),
            pltpu.VMEM((n, 1, 2 * own), F32),
            pltpu.VMEM((n, 1, 2 * own), F32),
            pltpu.VMEM((own, wide_txt), F32),
            pltpu.VMEM((1, 2 * own), F32),
            pltpu.VMEM((2 * fast, slow * chunk, shared), F32),
            pltpu.VMEM((fast, slow * chunk, shared), jnp.int16),
            pltpu.VMEM((fast, slow * chunk, shared), jnp.int16),
            pltpu.VMEM((fast - 1, slow * chunk, shared), jnp.int16),
            pltpu.VMEM((fast - 1, slow * chunk, shared), jnp.int16),
            pltpu.VMEM((slow, chunk, shared), F32),
            pltpu.VMEM((slow - 1, chunk, shared), jnp.int16),
            pltpu.VMEM((slow - 1, chunk, shared), jnp.int16),
            pltpu.VMEM((fast, 1, shared), F32),
            pltpu.VMEM((fast, 1, shared), F32),
            pltpu.VMEM((fast - 1, 1, shared), F32),
            pltpu.VMEM((fast - 1, 1, shared), F32),
            pltpu.VMEM((slow - 1, 1, shared), F32),
            pltpu.VMEM((slow - 1, 1, shared), F32),
            dma((n - 1,)),
            dma((n,)),
            dma((2,)),
            dma((2,)),
            dma((4, fast)),
            dma((4, fast - 1)),
            dma((4, slow - 1)),
            dma((n - 1,)),
            dma((n,)),
            dma((2,)),
        ],
        compiler_params=pltpu.CompilerParams(
            collective_id=0, has_side_effects=True, vmem_limit_bytes=48 * 2**20
        ),
    )(image_feats, text_feats, class_ids.reshape(1, own), w_img, w_txt)
    grads = full.astype(F32) * scale
    grads = grads.reshape(2 * fast, slow * chunk, shared)[:, :part].reshape(-1, shared)
    return loss.reshape(1), grads[:wide_img], grads[wide_img:]


def solution(mesh):
    return jax.shard_map(
        functools.partial(body, mesh.shape["blk"]),
        mesh=mesh,
        in_specs=(
            P(("groups", "blk"), None),
            P(("groups", "blk"), None),
            P(("groups", "blk")),
            P(),
            P(),
        ),
        out_specs=(P("groups"), P("groups", None), P("groups", None)),
        check_vma=False,
    )
```

time: 229 us -> 92.1 us (0.40)
  waiting for transfers between devices: 115 us -> 0 us
  Pallas kernels: 0 us -> 81 us
  blocking collectives: 56.6 us -> 0 us
  matrix products: 29.3 us -> 0 us
  between operations: 16.6 us -> 2.36 us
  loops' own time: 2.63 us -> 0 us
    psum x1 -> x0, waiting for transfers between devices: 97.5 us -> none  [body(): lax.psum((loss_sum, image_grad, text_first - text_second), 'blk')]
    pallas_call x0 -> x1, Pallas kernels: none -> 81 us  [body(): pl.pallas_call(functools.partial(kernel, n), out_shape=(jax.ShapeDtypeStr...]
    psum x1 -> x0, blocking collectives: 33.4 us -> none  [body(): lax.psum((loss_sum, image_grad, text_first - text_second), 'blk')]
    dot_general x20 -> x0, matrix products: 29.3 us -> none  [the longest x4 8.88 us: visit(): jnp.dot(query_rows, shard_rows.T, preferred_element_type=jnp.float32)]
    all_gather x1 -> x0, blocking collectives: 23.2 us -> none  [body(): lax.all_gather(class_ids, 'blk', axis=0, tiled=True)]
    all_gather x1 -> x0, waiting for transfers between devices: 17.4 us -> none  [body(): lax.all_gather(scaled_txt, 'blk', axis=0, tiled=True)]
    another operation x1 -> x0, loops' own time: 2.63 us -> none  [body(): final_state = lax.fori_loop(0, span_count, loop_step, start_carry)]
    slice x0 -> x2, local copies, waits for them, and re-layouts: none -> 2.3 us  [body(): return (loss.reshape(1), grads[:wide_img], grads[wide_img:])]
  transfers between devices with their start and end apart: 2 -> 0, of which waited for: 2 -> 0; matrix products, arithmetic and copies ran while one was open for 1% -> 0% of each run, Pallas kernels for 0% -> 0%
where the time goes in v1:
time: 92.1 us; the launch traced here: 90.7 us
  Pallas kernels  81 us (88%)
  local copies, waits for them, and re-layouts  6.96 us (8%)
  between operations  2.36 us (3%)
    pallas_call x1, Pallas kernels, body(): pl.pallas_call(functools.partial(kernel, n), out_shape=(jax.ShapeDtypeStr...  81 us
    unnamed x11, local copies, waits for them, and re-layouts  4.66 us
    slice x2, local copies, waits for them, and re-layouts, body(): return (loss.reshape(1), grads[:wide_img], grads[wide_img:])  2.3 us

profile of v1, /device:TPU:0, one launch (start us, length us, event | category | flops | bytes accessed | tf_op | source)
XLA Modules:
  0.0 90.7 jit_solution(17468718110921899288)
XLA Ops:
  0.6 0.0 copy-start
  0.6 1.1 %copy-done = bf16[768,512]{1,0:T(8,128)(2,1)S(1)} copy-done((bf16[768,512]{1,0:T(8,128)(2,1)S(1)}, bf16[768,512]{1,0:T(8,128)(2,1)}, u32[]{:S(2)}) %copy-start) | copy-done | bytes 786456
  1.8 0.0 copy-start.1
  1.8 1.0 %copy-done.1 = bf16[512,512]{1,0:T(8,128)(2,1)S(1)} copy-done((bf16[512,512]{1,0:T(8,128)(2,1)S(1)}, bf16[512,512]{1,0:T(8,128)(2,1)}, u32[]{:S(2)}) %copy-start.1) | copy-done | bytes 524312
  2.8 0.0 copy-start.2
  2.8 0.9 %copy-done.2 = bf16[128,768]{1,0:T(8,128)(2,1)S(1)} copy-done((bf16[128,768]{1,0:T(8,128)(2,1)S(1)}, bf16[128,768]{1,0:T(8,128)(2,1)}, u32[]{:S(2)}) %copy-start.2) | copy-done | bytes 196632
  3.7 0.0 copy-start.3
  3.7 0.9 copy-done.3
  4.6 0.0 copy-start.4
  4.6 0.7 copy-done.4
  5.3 81.0 %shard_map.76 = (f32[1,1]{1,0:T(1,128)}, s16[16,80,512]{2,1,0:T(8,128)(2,1)S(1)}, f32[16,1,512]{2,1,0:T(1,128)S(1)}) custom-call(bf16[128,768]{1,0:T(8,128)(2,1)S(1)} %copy-done.2, bf16[128,512]{1,0:T(8,128)(2,1)S(1)} %copy-done.3, s32[1,128]{1,0:T(1,128)S(1)} %bitcast.6, bf16[768,512]{1,0:T(8,128)(2,1)S(1)} %copy-done, bf16[512,512]{1,0:T(8,128)(2,1)S(1)} %copy-done.1), custom_call_target="tpu_custom_call" | custom-call | tf_op jit(solution)/shard_map/pallas_call | solution.py:364
  86.3 0.4 convert_multiply_fusion
  86.7 1.0 %slice.9 = f32[512,512]{1,0:T(8,128)} slice(f32[1280,512]{1,0:T(8,128)S(1)} %bitcast.7), slice={[768:1280], [0:512]} | slice | bytes 2097152 | tf_op jit(solution)/shard_map/slice | solution.py:411
  87.8 1.3 %slice.8 = f32[768,512]{1,0:T(8,128)} slice(f32[1280,512]{1,0:T(8,128)S(1)} %bitcast.8), slice={[0:768], [0:512]} | slice | bytes 3145728 | tf_op jit(solution)/shard_map/slice | solution.py:411
  (1 shorter events, 0.0 us)
Async XLA Ops:
  0.6 1.1 %copy-start = (bf16[768,512]{1,0:T(8,128)(2,1)S(1)}, bf16[768,512]{1,0:T(8,128)(2,1)}, u32[]{:S(2)}) copy-start(bf16[768,512]{1,0:T(8,128)(2,1)} %w_img_ref.1) | copy-start | bytes 2359300
  1.8 1.0 %copy-start.1 = (bf16[512,512]{1,0:T(8,128)(2,1)S(1)}, bf16[512,512]{1,0:T(8,128)(2,1)}, u32[]{:S(2)}) copy-start(bf16[512,512]{1,0:T(8,128)(2,1)} %w_txt_ref.1) | copy-start | bytes 1572868
  2.8 0.9 %copy-start.2 = (bf16[128,768]{1,0:T(8,128)(2,1)S(1)}, bf16[128,768]{1,0:T(8,128)(2,1)}, u32[]{:S(2)}) copy-start(bf16[128,768]{1,0:T(8,128)(2,1)} %img_ref.1) | copy-start | bytes 589828
  3.7 0.9 copy-start.3
  4.6 0.7 copy-start.4

commit v2 on v0

v2 whole, which is shorter than its diff:
```python
import functools

import jax
import jax.numpy as jnp
from jax import lax
from jax.experimental import pallas as pl
from jax.experimental.pallas import tpu as pltpu
from jax.sharding import PartitionSpec as P

LOGIT_SCALE = 10.0
LOGIT_BIAS = -10.0
NORM_EPS = 1e-06
F32 = jnp.float32
BF16 = jnp.bfloat16
LEVELS = 32767.0


LANES = 128
HEAD = 16
SLOW = 4


def padded(rows):
    return -(-rows // 16) * 16


def split(value):
    high = value.astype(BF16)
    return high, (value - high.astype(F32)).astype(BF16)


def pack(value, rows):
    peak = jnp.maximum(jnp.max(jnp.abs(value), axis=0, keepdims=True), 1e-30)
    power = jnp.ceil(jnp.log2(peak * (1.0001 / LEVELS)))
    levels = jnp.round(value * jnp.exp2(-power))
    parts = [levels]
    if rows > value.shape[0]:
        parts.append(jnp.zeros((rows - value.shape[0], LANES), F32))
    parts.append(jnp.broadcast_to(power, (HEAD, LANES)))
    return jnp.concatenate(parts).astype(jnp.int32).astype(jnp.int16)


def unpack(message, part, rows):
    wide = message.astype(jnp.int32).astype(F32)
    return wide[:part] * jnp.exp2(wide[rows:rows + 1])


def dot_nn(a, b):
    return jnp.dot(a, b, preferred_element_type=F32)


def dot_nt(a, b):
    return lax.dot_general(a, b, (((1,), (1,)), ((), ())), preferred_element_type=F32)


def dot_tn(a, b):
    return lax.dot_general(a, b, (((0,), (0,)), ((), ())), preferred_element_type=F32)


def as_column(row):
    length = row.shape[1]
    return jnp.broadcast_to(row, (length, length)).T[:, :1]


def loop(first, last, use):
    def step(i, carry):
        use(i)
        return carry

    lax.fori_loop(first, last, step, 0)


def kernel(
    n,
    img_hbm, txt_hbm, ids_hbm, w_img_hbm, w_txt_hbm,
    loss_ref, full_ref,
    w_img_ref, w_txt_ref, txt_ref, img_all, txt_all, ids_rows, ids_cols,
    img_turned, across_high, across_low, unit_high, unit_low, inv_all, query, across,
    row_ids, txt_turned, text_high, text_low, dots, loss_acc, loss_slow, loss_plane,
    grads, out_core, in_core, out_fast, in_fast, out_slow, in_slow,
    local_sem, img_send, img_recv, txt_sem, ids_sem, loss_sem,
    core_sem, fast_sem, slow_sem, full_send, full_recv,
):
    fast = n // (2 * SLOW)
    plane = 2 * fast
    own, wide_img = img_all.shape[1:]
    wide_txt = txt_all.shape[2]
    blocks, size = query.shape[:2]
    part = (wide_img + wide_txt) // plane
    rows = full_ref.shape[1] - HEAD
    per = size // own
    total_rows = n * own
    me = lax.axis_index("blk")
    mp = lax.rem(me, plane)
    mc = lax.rem(me, 2)
    my = mp // 2
    mz = me // plane

    def device(z, y, c):
        return (z * fast + y) * 2 + c

    def along(d):
        return device(lax.rem(mz + d, SLOW), my, mc)

    def across_fast(d):
        return device(mz, lax.rem(my + d, fast), mc)

    def in_plane(d):
        return mz * plane + lax.rem(mp + d, plane)

    sibling = device(mz, my, 1 - mc)

    barrier = pltpu.get_barrier_semaphore()
    for d in range(1, SLOW):
        pl.semaphore_signal(barrier, inc=1, device_id={"blk": along(d)})
    loop(1, plane, lambda d: pl.semaphore_signal(barrier, inc=1, device_id={"blk": in_plane(d)}))

    loads = [
        pltpu.make_async_copy(a, b, local_sem.at[k])
        for k, (a, b) in enumerate([
            (txt_hbm, txt_ref), (w_txt_hbm, w_txt_ref), (img_hbm, img_all.at[mp]),
            (w_img_hbm, w_img_ref), (ids_hbm, ids_rows.at[mp]), (ids_hbm, ids_cols.at[mz]),
        ])
    ]
    for load in loads:
        load.start()

    def remote(src, dst, send, recv, where):
        return pltpu.make_async_remote_copy(
            src_ref=src, dst_ref=dst, send_sem=send, recv_sem=recv, device_id={"blk": where}
        )

    def img_copy(y, c, dst, k):
        slot = img_all.at[y * 2 + c]
        return remote(slot, slot, img_send.at[k], img_recv.at[y * 2 + c], dst)

    def txt_copy(z, d):
        return remote(txt_all.at[z], txt_all.at[z], txt_sem.at[0, d], txt_sem.at[1, z], along(d))

    def ids_row_copy(d):
        slot = ids_rows.at[mp]
        return remote(slot, slot, ids_sem.at[0], ids_sem.at[1], in_plane(d))

    def ids_col_copy(d):
        slot = ids_cols.at[mz]
        return remote(slot, slot, ids_sem.at[2], ids_sem.at[3], along(d))

    loads[0].wait()
    loads[1].wait()
    proj_txt = dot_nn(txt_ref[...], w_txt_ref[...])
    inv_txt = lax.rsqrt(jnp.sum(proj_txt * proj_txt, axis=1, keepdims=True) + NORM_EPS)
    txt_all[mz] = (txt_ref[...].astype(F32) * inv_txt).astype(BF16)
    for load in loads[2:]:
        load.wait()
    pl.semaphore_wait(barrier, SLOW + plane - 2)

    for d in range(1, SLOW):
        txt_copy(mz, d).start()
    loop(1, fast, lambda d: img_copy(my, mc, across_fast(d), d).start())
    img_copy(my, mc, sibling, 0).start()
    for d in range(1, SLOW):
        ids_col_copy(d).start()
    loop(1, plane, lambda d: ids_row_copy(d).start())

    loss_acc[...] = jnp.zeros_like(loss_acc)

    def pass_on(d):
        y = lax.rem(my + d, fast)
        img_copy(y, mc, sibling, 0).wait_recv()
        img_copy(y, mc, sibling, fast - 1 + d).start()

    loop(1, fast, pass_on)
    loop(0, fast, lambda d: img_copy(d, 1 - mc, sibling, 0).wait_recv())
    remote(
        ids_rows.at[pl.ds(0, plane - 1)], ids_rows.at[pl.ds(0, plane - 1)],
        ids_sem.at[0], ids_sem.at[1], sibling,
    ).wait()

    def project(block):
        img = img_all[pl.ds(block * per, per)].reshape(size, wide_img)
        proj_img = dot_nn(img, w_img_ref[...])
        inv_img = lax.rsqrt(jnp.sum(proj_img * proj_img, axis=1, keepdims=True) + NORM_EPS)
        unit_img = proj_img * inv_img
        high, low = split(unit_img)
        query[block] = (dot_nt(high, w_txt_ref[...]) + dot_nt(low, w_txt_ref[...])).astype(BF16)
        unit_high[block], unit_low[block] = high, low
        inv_all[block] = inv_img
        img_turned[block] = img.T
        across[block] = jnp.zeros((size, wide_txt), F32)
        row_ids[block] = jnp.concatenate(
            [as_column(ids_rows[block * per + i].astype(F32)) for i in range(per)]
        )

    loop(0, blocks, project)
    remote(
        ids_cols.at[pl.ds(0, SLOW - 1)], ids_cols.at[pl.ds(0, SLOW - 1)],
        ids_sem.at[2], ids_sem.at[3], sibling,
    ).wait()

    def visit(d):
        z = lax.rem(mz + d, SLOW)

        @pl.when(d > 0)
        def _():
            txt_copy(z, 0).wait_recv()

        text = txt_all[z]
        ids = ids_cols[z].astype(F32)
        dots[...] = jnp.zeros_like(dots)

        def tile(block):
            cosine = dot_nt(query[block], text)
            logits = LOGIT_SCALE * cosine + LOGIT_BIAS
            labels = jnp.where(row_ids[block] == ids, 1.0, -1.0).astype(F32)
            margin = -labels * logits
            decay = jnp.exp(-jnp.abs(margin))
            terms = jnp.maximum(margin, 0.0) + jnp.log1p(decay)
            loss_acc[...] += jnp.sum(terms, axis=0, keepdims=True)
            gate = jnp.where(margin >= 0.0, 1.0, decay) / (1.0 + decay)
            slope = (-LOGIT_SCALE / total_rows) * labels * gate
            across[block] += dot_nn(slope.astype(BF16), text)
            dots[...] += jnp.sum(slope * cosine, axis=0, keepdims=True)

        loop(0, blocks, tile)
        unit_txt = dot_nn(text, w_txt_ref[...])
        place = pl.ds(d * own, own)
        text_high[place], text_low[place] = split(-unit_txt * as_column(dots[...]))
        txt_turned[d] = text.T

    loop(0, SLOW, visit)
    d_high = query
    loop(0, 2 * fast - 1, lambda k: img_copy(my, mc, sibling, k).wait_send())

    def loss_along(d):
        return remote(loss_acc, loss_slow.at[mz], loss_sem.at[0, 0], loss_sem.at[0, 1], along(d))

    def loss_over(d):
        slot = loss_plane.at[mp]
        return remote(slot, slot, loss_sem.at[1, 0], loss_sem.at[1, 1], in_plane(d))

    for d in range(1, SLOW):
        loss_along(d).start()
    loss_slow[mz] = loss_acc[...]

    def turn(block):
        high, low = split(across[block])
        d_unit_img = dot_nn(high, w_txt_ref[...]) + dot_nn(low, w_txt_ref[...])
        unit_img = unit_high[block].astype(F32) + unit_low[block].astype(F32)
        d_proj_img = inv_all[block] * (
            d_unit_img - unit_img * jnp.sum(unit_img * d_unit_img, axis=1, keepdims=True)
        )
        d_high[block], low_part = split(d_proj_img)
        img_all[pl.ds(block * per, per), :, pl.ds(0, d_high.shape[2])] = low_part.reshape(per, own, -1)
        across_high[block], across_low[block] = high.T, low.T

    loop(0, blocks, turn)

    def core_copy(i):
        return remote(out_core.at[i], in_core.at[i], core_sem.at[0, i], core_sem.at[1, i], sibling)

    def fast_copy(i, d):
        return remote(
            out_fast.at[i, d - 1], in_fast.at[i, d - 1],
            fast_sem.at[0, i, d - 1], fast_sem.at[1, i, d - 1], across_fast(d),
        )

    def slow_copy(i):
        return remote(
            out_slow.at[i], in_slow.at[i], slow_sem.at[0, i], slow_sem.at[1, i], along(i + 1)
        )

    def make(i):
        first = pl.multiple_of(lax.rem(mz + 1 + i, SLOW) * LANES, LANES)
        columns = pl.ds(first, LANES)

        def add(block, sums):
            image, text = sums
            d_low = img_all[pl.ds(block * per, per), :, columns].reshape(size, LANES)
            image = image + dot_nn(img_turned[block], d_high[block, :, columns])
            image = image + dot_nn(img_turned[block], d_low)
            text = text + dot_nn(across_high[block], unit_high[block, :, columns])
            text = text + dot_nn(across_low[block], unit_high[block, :, columns])
            text = text + dot_nn(across_high[block], unit_low[block, :, columns])
            return image, text

        text = jnp.zeros((wide_txt, LANES), F32)
        for d in range(SLOW):
            place = pl.ds(d * own, own)
            text = text + dot_nn(txt_turned[d], text_high[place, columns])
            text = text + dot_nn(txt_turned[d], text_low[place, columns])
        sums = jnp.zeros((wide_img, LANES), F32), text
        sums = add(0, sums) if blocks == 1 else lax.fori_loop(0, blocks, add, sums)
        grads[i] = jnp.concatenate(sums).reshape(plane, part, LANES)

        def other(j):
            out_core[i, j] = pack(grads[i, (1 - mc) * fast + j], rows)

        loop(0, fast, other)
        core_copy(i).start()

    def summed(i, j):
        return grads[i, mc * fast + j] + unpack(in_core[i, j], part, rows)

    def pass_fast(i):
        core_copy(i).wait_recv()

        def one(d):
            out_fast[i, d - 1] = pack(summed(i, lax.rem(my + d, fast)), rows)
            fast_copy(i, d).start()

        loop(1, fast, one)

    def total(i):
        def one(d, value):
            fast_copy(i, d).wait_recv()
            return value + unpack(in_fast[i, d - 1], part, rows)

        return lax.fori_loop(1, fast, one, summed(i, my))

    def pass_slow(i):
        out_slow[i] = pack(total(i), rows)
        slow_copy(i).start()

    for i in range(SLOW + 2):
        if i < SLOW:
            make(i)
        if 1 <= i <= SLOW:
            pass_fast(i - 1)
        if 2 <= i <= SLOW:
            pass_slow(i - 2)

    remote(
        loss_slow.at[pl.ds(0, SLOW - 1)], loss_slow.at[pl.ds(0, SLOW - 1)],
        loss_sem.at[0, 0], loss_sem.at[0, 1], sibling,
    ).wait()
    loss_plane[mp] = jnp.sum(loss_slow[...], axis=0)
    loop(1, plane, lambda d: loss_over(d).start())

    value = total(SLOW - 1)
    for i in range(SLOW - 1):
        slow_copy(i).wait_recv()
        value = value + unpack(in_slow[i], part, rows)

    half = (rows + HEAD) // 32 * 16
    halves = [(0, half), (half, rows + HEAD - half)]

    def full_copy(h, z, y, c, dst, k):
        first, count = halves[h]
        slot = full_ref.at[(c * fast + y) * SLOW + z, pl.ds(first, count)]
        return remote(slot, slot, full_send.at[h, k], full_recv.at[h, device(z, y, c)], dst)

    full_ref[(mc * fast + my) * SLOW + mz] = pack(value, rows)
    base = SLOW - 1 + SLOW * (fast - 1)

    def forward(h, dz):
        z = lax.rem(mz + dz, SLOW)

        def one(d):
            k = SLOW - 1 + dz * (fast - 1) + d - 1
            full_copy(h, z, my, mc, across_fast(d), k).start()

        loop(1, fast, one)
        full_copy(h, z, my, mc, sibling, base + dz * fast).start()

    for h in range(2):
        for d in range(1, SLOW):
            full_copy(h, mz, my, mc, along(d), d - 1).start()
        forward(h, 0)
    for h in range(2):
        for dz in range(1, SLOW):
            full_copy(h, lax.rem(mz + dz, SLOW), my, mc, sibling, 0).wait_recv()
            forward(h, dz)

    for h in range(2):
        for dz in range(SLOW):
            z = lax.rem(mz + dz, SLOW)

            def one(d):
                y = lax.rem(my + d, fast)
                full_copy(h, z, y, mc, sibling, 0).wait_recv()
                full_copy(h, z, y, mc, sibling, base + dz * fast + d).start()

            loop(1, fast, one)

    remote(
        loss_plane.at[pl.ds(0, plane - 1)], loss_plane.at[pl.ds(0, plane - 1)],
        loss_sem.at[1, 0], loss_sem.at[1, 1], sibling,
    ).wait()
    loss_ref[...] = jnp.sum(jnp.sum(loss_plane[...], axis=0), axis=1, keepdims=True) / total_rows

    for h in range(2):
        for z in range(SLOW):
            loop(0, fast, lambda y: full_copy(h, z, y, 1 - mc, sibling, 0).wait_recv())
    for d in range(1, SLOW):
        txt_copy(mz, d).wait_send()
    for i in range(SLOW):
        core_copy(i).wait_send()
        loop(1, fast, lambda d: fast_copy(i, d).wait_send())
    for i in range(SLOW - 1):
        slow_copy(i).wait_send()
    for h in range(2):
        loop(0, n - 1, lambda k: full_copy(h, mz, my, mc, sibling, k).wait_send())


def body(n, image_feats, text_feats, class_ids, w_img, w_txt):
    own, wide_img = image_feats.shape
    wide_txt = text_feats.shape[1]
    shared = w_img.shape[1]
    fast = n // (2 * SLOW)
    plane = 2 * fast
    part = (wide_img + wide_txt) // plane
    rows = padded(part)
    tall = rows + HEAD
    size = min(plane, 4) * own
    blocks = plane * own // size
    columns = SLOW * own
    vmem = pltpu.VMEM
    dma = pltpu.SemaphoreType.DMA
    loss, full = pl.pallas_call(
        functools.partial(kernel, n),
        out_shape=(
            jax.ShapeDtypeStruct((1, 1), F32),
            jax.ShapeDtypeStruct((n, tall, LANES), jnp.int16),
        ),
        in_specs=[pl.BlockSpec(memory_space=pl.ANY)] * 5,
        out_specs=(pl.BlockSpec(memory_space=pltpu.VMEM),) * 2,
        scratch_shapes=[
            vmem(w_img.shape, BF16),
            vmem(w_txt.shape, BF16),
            vmem(text_feats.shape, BF16),
            vmem((plane, own, wide_img), BF16),
            vmem((SLOW, own, wide_txt), BF16),
            vmem((plane, 1, own), jnp.int32),
            vmem((SLOW, 1, own), jnp.int32),
            vmem((blocks, wide_img, size), BF16),
            vmem((blocks, wide_txt, size), BF16),
            vmem((blocks, wide_txt, size), BF16),
            vmem((blocks, size, shared), BF16),
            vmem((blocks, size, shared), BF16),
            vmem((blocks, size, 1), F32),
            vmem((blocks, size, wide_txt), BF16),
            vmem((blocks, size, wide_txt), F32),
            vmem((blocks, size, 1), F32),
            vmem((SLOW, wide_txt, own), BF16),
            vmem((columns, shared), BF16),
            vmem((columns, shared), BF16),
            vmem((1, own), F32),
            vmem((1, own), F32),
            vmem((SLOW, 1, own), F32),
            vmem((plane, 1, own), F32),
            vmem((SLOW, plane, part, LANES), F32),
            vmem((SLOW, fast, tall, LANES), jnp.int16),
            vmem((SLOW, fast, tall, LANES), jnp.int16),
            vmem((SLOW, fast - 1, tall, LANES), jnp.int16),
            vmem((SLOW, fast - 1, tall, LANES), jnp.int16),
            vmem((SLOW - 1, tall, LANES), jnp.int16),
            vmem((SLOW - 1, tall, LANES), jnp.int16),
            dma((6,)),
            dma((2 * fast - 1,)),
            dma((plane,)),
            dma((2, SLOW)),
            dma((4,)),
            dma((2, 2)),
            dma((2, SLOW)),
            dma((2, SLOW, fast - 1)),
            dma((2, SLOW - 1)),
            dma((2, n - 1)),
            dma((2, n)),
        ],
        compiler_params=pltpu.CompilerParams(
            collective_id=0, has_side_effects=True, vmem_limit_bytes=(40 if blocks == 1 else 60) * 2**20
        ),
    )(image_feats, text_feats, class_ids.reshape(1, own), w_img, w_txt)
    full = full.reshape(plane, SLOW, tall, LANES)
    scale = jnp.exp2(full[:, :, rows].astype(F32))
    grads = full[:, :, :part].astype(F32) * scale[:, :, None]
    grads = grads.transpose(0, 2, 1, 3).reshape(-1, shared)
    return loss.reshape(1), grads[:wide_img], grads[wide_img:]


def solution(mesh):
    return jax.shard_map(
        functools.partial(body, mesh.shape["blk"]),
        mesh=mesh,
        in_specs=(
            P(("groups", "blk"), None),
            P(("groups", "blk"), None),
            P(("groups", "blk")),
            P(),
            P(),
        ),
        out_specs=(P("groups"), P("groups", None), P("groups", None)),
        check_vma=False,
    )
```

time: 229 us -> 63.4 us (0.28)
  waiting for transfers between devices: 115 us -> 0 us
  blocking collectives: 56.6 us -> 0 us
  Pallas kernels: 0 us -> 51.3 us
  matrix products: 29.3 us -> 0 us
  between operations: 16.6 us -> 2.37 us
  loops' own time: 2.63 us -> 0 us
    psum x1 -> x0, waiting for transfers between devices: 97.5 us -> none  [body(): lax.psum((loss_sum, image_grad, text_first - text_second), 'blk')]
    pallas_call x0 -> x1, Pallas kernels: none -> 51.3 us  [body(): pl.pallas_call(functools.partial(kernel, n), out_shape=(jax.ShapeDtypeStr...]
    psum x1 -> x0, blocking collectives: 33.4 us -> none  [body(): lax.psum((loss_sum, image_grad, text_first - text_second), 'blk')]
    dot_general x20 -> x0, matrix products: 29.3 us -> none  [the longest x4 8.88 us: visit(): jnp.dot(query_rows, shard_rows.T, preferred_element_type=jnp.float32)]
    all_gather x1 -> x0, blocking collectives: 23.2 us -> none  [body(): lax.all_gather(class_ids, 'blk', axis=0, tiled=True)]
    all_gather x1 -> x0, waiting for transfers between devices: 17.4 us -> none  [body(): lax.all_gather(scaled_txt, 'blk', axis=0, tiled=True)]
    another operation x1 -> x0, loops' own time: 2.63 us -> none  [body(): final_state = lax.fori_loop(0, span_count, loop_step, start_carry)]
    slice x0 -> x2, local copies, waits for them, and re-layouts: none -> 2.3 us  [body(): return (loss.reshape(1), grads[:wide_img], grads[wide_img:])]
  transfers between devices with their start and end apart: 2 -> 0, of which waited for: 2 -> 0; matrix products, arithmetic and copies ran while one was open for 1% -> 0% of each run, Pallas kernels for 0% -> 0%
where the time goes in v2:
time: 63.4 us; the launch traced here: 63 us
  Pallas kernels  51.3 us (81%)
  local copies, waits for them, and re-layouts  8.88 us (14%)
  between operations  2.37 us (4%)
    pallas_call x1, Pallas kernels, body(): pl.pallas_call(functools.partial(kernel, n), out_shape=(jax.ShapeDtypeStr...  51.3 us
    unnamed x11, local copies, waits for them, and re-layouts  4.89 us
    slice x2, local copies, waits for them, and re-layouts, body(): return (loss.reshape(1), grads[:wide_img], grads[wide_img:])  2.3 us
    transpose x1, local copies, waits for them, and re-layouts, body(): grads = grads.transpose(0, 2, 1, 3).reshape(-1, shared)  1.69 us

profile of v2, /device:TPU:0, one launch (start us, length us, event | category | flops | bytes accessed | tf_op | source)
XLA Modules:
  0.0 63.0 jit_solution(13270116149330576696)
XLA Ops:
  0.6 0.0 copy-start
  0.6 1.1 %copy-done = bf16[768,512]{1,0:T(8,128)(2,1)S(1)} copy-done((bf16[768,512]{1,0:T(8,128)(2,1)S(1)}, bf16[768,512]{1,0:T(8,128)(2,1)}, u32[]{:S(2)}) %copy-start) | copy-done | bytes 786456
  1.8 0.0 copy-start.1
  1.8 1.0 %copy-done.1 = bf16[512,512]{1,0:T(8,128)(2,1)S(1)} copy-done((bf16[512,512]{1,0:T(8,128)(2,1)S(1)}, bf16[512,512]{1,0:T(8,128)(2,1)}, u32[]{:S(2)}) %copy-start.1) | copy-done | bytes 524312
  2.8 0.0 copy-start.2
  2.8 0.9 %copy-done.2 = bf16[128,768]{1,0:T(8,128)(2,1)S(1)} copy-done((bf16[128,768]{1,0:T(8,128)(2,1)S(1)}, bf16[128,768]{1,0:T(8,128)(2,1)}, u32[]{:S(2)}) %copy-start.2) | copy-done | bytes 196632
  3.7 0.0 copy-start.3
  3.7 0.9 %copy-done.3 = bf16[128,512]{1,0:T(8,128)(2,1)S(1)} copy-done((bf16[128,512]{1,0:T(8,128)(2,1)S(1)}, bf16[128,512]{1,0:T(8,128)(2,1)}, u32[]{:S(2)}) %copy-start.3) | copy-done | bytes 131096
  4.6 0.0 copy-start.4
  4.6 0.7 %copy-done.4 = s32[128]{0:T(128)S(1)} copy-done((s32[128]{0:T(128)S(1)}, s32[128]{0:T(128)}, u32[]{:S(2)}) %copy-start.4) | copy-done | bytes 536
  5.3 51.3 %shard_map.76 = (f32[1,1]{1,0:T(1,128)}, s16[16,336,128]{2,1,0:T(8,128)(2,1)S(1)}) custom-call(bf16[128,768]{1,0:T(8,128)(2,1)S(1)} %copy-done.2, bf16[128,512]{1,0:T(8,128)(2,1)S(1)} %copy-done.3, s32[1,128]{1,0:T(1,128)S(1)} %bitcast.13, bf16[768,512]{1,0:T(8,128)(2,1)S(1)} %copy-done, bf16[512,512]{1,0:T(8,128)(2,1)S(1)} %copy-done.1), custom_call_target="tpu_custom_call" | custom-call | tf_op jit(solution)/shard_map/pallas_call | solution.py:419
  56.7 0.4 multiply_bitcast_fusion
  57.1 1.7 %copy.8 = f32[4,320,4,128]{3,2,1,0:T(4,128)S(1)} copy(f32[4,320,4,128]{3,1,2,0:T(8,128)S(1)} %multiply_bitcast_fusion) | data formatting | bytes 5242880 | tf_op jit(solution)/shard_map/transpose | solution.py:477
  58.8 0.2 copy.11
  59.0 1.0 %slice.19 = f32[512,512]{1,0:T(8,128)} slice(f32[1280,512]{1,0:T(8,128)S(1)} %bitcast.14), slice={[768:1280], [0:512]} | slice | bytes 2097152 | tf_op jit(solution)/shard_map/slice | solution.py:478
  60.1 1.3 %slice.18 = f32[768,512]{1,0:T(8,128)} slice(f32[1280,512]{1,0:T(8,128)S(1)} %bitcast.15), slice={[0:768], [0:512]} | slice | bytes 3145728 | tf_op jit(solution)/shard_map/slice | solution.py:478
  (1 shorter events, 0.0 us)
Async XLA Ops:
  0.6 1.1 %copy-start = (bf16[768,512]{1,0:T(8,128)(2,1)S(1)}, bf16[768,512]{1,0:T(8,128)(2,1)}, u32[]{:S(2)}) copy-start(bf16[768,512]{1,0:T(8,128)(2,1)} %w_img_hbm.1) | copy-start | bytes 2359300
  1.8 1.0 %copy-start.1 = (bf16[512,512]{1,0:T(8,128)(2,1)S(1)}, bf16[512,512]{1,0:T(8,128)(2,1)}, u32[]{:S(2)}) copy-start(bf16[512,512]{1,0:T(8,128)(2,1)} %w_txt_hbm.1) | copy-start | bytes 1572868
  2.8 0.9 %copy-start.2 = (bf16[128,768]{1,0:T(8,128)(2,1)S(1)}, bf16[128,768]{1,0:T(8,128)(2,1)}, u32[]{:S(2)}) copy-start(bf16[128,768]{1,0:T(8,128)(2,1)} %img_hbm.1) | copy-start | bytes 589828
  3.7 0.9 %copy-start.3 = (bf16[128,512]{1,0:T(8,128)(2,1)S(1)}, bf16[128,512]{1,0:T(8,128)(2,1)}, u32[]{:S(2)}) copy-start(bf16[128,512]{1,0:T(8,128)(2,1)} %txt_hbm.1) | copy-start | bytes 393220
  4.6 0.7 %copy-start.4 = (s32[128]{0:T(128)S(1)}, s32[128]{0:T(128)}, u32[]{:S(2)}) copy-start(s32[128]{0:T(128)} %param.7) | copy-start | bytes 1540

commit v3 on v2

--- a/solution.py
+++ b/solution.py
@@ -468,7 +468,7 @@
             dma((2, n)),
         ],
         compiler_params=pltpu.CompilerParams(
-            collective_id=0, has_side_effects=True, vmem_limit_bytes=(40 if blocks == 1 else 60) * 2**20
+            collective_id=0, has_side_effects=True, vmem_limit_bytes=(63 if blocks == 1 else 60) * 2**20
         ),
     )(image_feats, text_feats, class_ids.reshape(1, own), w_img, w_txt)
     full = full.reshape(plane, SLOW, tall, LANES)

time: 63.4 us -> 61.6 us (0.972)
  local copies, waits for them, and re-layouts: 8.88 us -> 4.23 us
  other arithmetic: 0.46 us -> 2.54 us
  Pallas kernels: 51.3 us -> 52 us
    unnamed x11 -> x1, local copies, waits for them, and re-layouts: 4.89 us -> 0.24 us
    transpose x1, other arithmetic: 0.44 us -> 1.75 us  [body(): grads = grads.transpose(0, 2, 1, 3).reshape(-1, shared)]
    exp2 x1, other arithmetic: 0.03 us -> 0.78 us  [body(): scale = jnp.exp2(full[:, :, rows].astype(F32))]
    pallas_call x1, Pallas kernels: 51.3 us -> 52 us  [body(): pl.pallas_call(functools.partial(kernel, n), out_shape=(jax.ShapeDtypeStr...]
where the time goes in v3:
time: 61.6 us; the launch traced here: 61.2 us
  Pallas kernels  52 us (84%)
  local copies, waits for them, and re-layouts  4.23 us (7%)
  other arithmetic  2.54 us (4%)
  between operations  2.43 us (4%)
    pallas_call x1, Pallas kernels, body(): pl.pallas_call(functools.partial(kernel, n), out_shape=(jax.ShapeDtypeStr...  52 us
    slice x2, local copies, waits for them, and re-layouts, body(): return (loss.reshape(1), grads[:wide_img], grads[wide_img:])  2.3 us
    transpose x1, other arithmetic, body(): grads = grads.transpose(0, 2, 1, 3).reshape(-1, shared)  1.75 us
    transpose x1, local copies, waits for them, and re-layouts, body(): grads = grads.transpose(0, 2, 1, 3).reshape(-1, shared)  1.69 us

profile of v3, /device:TPU:0, one launch (start us, length us, event | category | flops | bytes accessed | tf_op | source)
XLA Modules:
  0.0 61.2 jit_solution(13989087875325538061)
XLA Ops:
  0.6 52.0 %shard_map.76 = (f32[1,1]{1,0:T(1,128)}, s16[16,336,128]{2,1,0:T(8,128)(2,1)}) custom-call(bf16[128,768]{1,0:T(8,128)(2,1)} %img_hbm.1, bf16[128,512]{1,0:T(8,128)(2,1)} %txt_hbm.1, s32[1,128]{1,0:T(1,128)} %bitcast.17, bf16[768,512]{1,0:T(8,128)(2,1)} %w_img_hbm.1, bf16[512,512]{1,0:T(8,128)(2,1)} %w_txt_hbm.1), custom_call_target="tpu_custom_call" | custom-call | tf_op jit(solution)/shard_map/pallas_call | solution.py:419
  52.6 0.8 %fusion.1 = f32[4,4,1,128]{3,2,1,0:T(1,128)S(1)} fusion(s16[4,4,336,128]{3,2,1,0:T(8,128)(2,1)} %bitcast.14), kind=kLoop, calls=%fused_computation.4 | loop fusion | flops 4096 | bytes 12288 | tf_op jit(solution)/shard_map/exp2 | solution.py:475
  53.4 1.8 %multiply_bitcast_fusion = f32[4,320,4,128]{3,1,2,0:T(8,128)S(1)} fusion(s16[4,4,336,128]{3,2,1,0:T(8,128)(2,1)} %bitcast.15, f32[4,4,128]{2,1,0:T(4,128)S(1)} %bitcast.16), kind=kLoop, calls=%fused_computation.1 | loop fusion | flops 1310720 | bytes 3940352 | tf_op jit(solution)/shard_map/transpose | solution.py:477
  55.2 1.7 %copy.8 = f32[4,320,4,128]{3,2,1,0:T(4,128)S(1)} copy(f32[4,320,4,128]{3,1,2,0:T(8,128)S(1)} %multiply_bitcast_fusion) | data formatting | bytes 5242880 | tf_op jit(solution)/shard_map/transpose | solution.py:477
  56.9 0.2 copy.11
  57.1 1.0 %slice.19 = f32[512,512]{1,0:T(8,128)} slice(f32[1280,512]{1,0:T(8,128)S(1)} %bitcast.11), slice={[768:1280], [0:512]} | slice | bytes 2097152 | tf_op jit(solution)/shard_map/slice | solution.py:478
  58.2 1.3 %slice.18 = f32[768,512]{1,0:T(8,128)} slice(f32[1280,512]{1,0:T(8,128)S(1)} %bitcast.12), slice={[0:768], [0:512]} | slice | bytes 3145728 | tf_op jit(solution)/shard_map/slice | solution.py:478
